TPU v7x, 32 devices: a whole 2x2x4 slice. The times are simulated.
32 devices in a mesh: gx: 8 (over y, x, core), gy: 4 (over z).
Axes of the slice: x: 2, y: 2, z: 4, core: 2. Of those that a mesh axis runs over, the one named last changes fastest.
Arguments:
- u_now: float32 [3, 6, 64, 512], P(None, None, 'gx', 'gy'), may hold values from -6 to 6
- u_prev: float32 [3, 6, 64, 512], P(None, None, 'gx', 'gy'), may hold values from -6 to 6
- lame_lambda: float32 [6, 64, 512], P(None, 'gx', 'gy'), may hold values from 0.5 to 1.5
- lame_mu: float32 [6, 64, 512], P(None, 'gx', 'gy'), may hold values from 0.3 to 1
- buoyancy: float32 [6, 64, 512], P(None, 'gx', 'gy'), may hold values from 0.5 to 1
- q_now: float32 [2048, 128], P(('gx', 'gy')), may hold values from -3 to 3
- q_prev: float32 [2048, 128], P(('gx', 'gy')), may hold values from -3 to 3
- archetype: int32 [2048], P(('gx', 'gy')), may hold values from 0 to 7
- stiffness: float32 [8, 128, 128], replicated, may hold values from -1.2 to 14, as said below
- couple: float32 [8, 3, 128], replicated, may hold values from -1.5 to 1.5
- counts: int32 [8, 4, 4], P('gx'), may hold values from 1 to 16, as said below
- footprint: int32 [8, 4, 256], P('gx', 'gy'), may hold values from 0 to 1023, as said below
Outputs:
- u_last: float32 [3, 6, 64, 512], P(None, None, 'gx', 'gy')
- u_before: float32 [3, 6, 64, 512], P(None, None, 'gx', 'gy')
- q_last: float32 [2048, 128], P(('gx', 'gy'))
- q_before: float32 [2048, 128], P(('gx', 'gy'))
Inputs may be any that keep to these rules, and one draw needn't show every extreme that they name: `stiffness`: symmetric, one matrix for each archetype. `counts`: at most 16; in every tile row some owner column receives 16 from every home column. `footprint`: the 4 cells of a slot form a 2 x 2 square of the home tile's surface, numbered x * 128 + y.
All inputs are finite; a program needn't handle non-finite values.
Results may differ from a plain program's by a relative error of at most 0.0001.
Values sent between devices are 32-bit elements; how exact they have to be, the bound alone decides.
A program may use at most 64 MiB of HBM per device.

v0:
```python
import jax
import jax.numpy as jnp
from jax import lax
from jax.sharding import PartitionSpec as P

FRAME_FREEDOMS = 128
FOOTPRINT_CELLS = 4
STEPS = 2
time_step = 0.25


def with_halo(array, sides, width):
    for axis, dim in sides:
        devices, length = (lax.axis_size(axis), array.shape[dim])
        up = [(i, (i + 1) % devices) for i in range(devices - 1)]
        down = [(j, i) for i, j in up]
        last = lax.slice_in_dim(array, length - width, length, axis=dim)
        initial = lax.slice_in_dim(array, 0, width, axis=dim)
        before = lax.ppermute(last, axis, up)
        after = lax.ppermute(initial, axis, down)
        array = jnp.concatenate([before, array, after], axis=dim)
    return array


def derive(padded, along):
    field = padded
    for other in (1, 2, 3):
        if other != along:
            field = lax.slice_in_dim(field, 2, field.shape[other] - 2, axis=other)
    length = field.shape[along] - 4

    def window(offset):
        return lax.slice_in_dim(field, offset, offset + length, axis=along)

    return (8.0 * (window(3) - window(1)) - (window(4) - window(0))) / 12.0


def stress_of(padded, lam_field, mu_field):
    grad_x = derive(padded, 2)
    grad_y = derive(padded, 3)
    grad_z = derive(padded, 1)
    trace = grad_x[0] + grad_y[1] + grad_z[2]
    return jnp.stack(
        [
            lam_field * trace + 2.0 * mu_field * grad_x[0],
            lam_field * trace + 2.0 * mu_field * grad_y[1],
            lam_field * trace + 2.0 * mu_field * grad_z[2],
            mu_field * (grad_y[0] + grad_x[1]),
            mu_field * (grad_z[0] + grad_x[2]),
            mu_field * (grad_z[1] + grad_y[2]),
        ]
    )


def divergence(padded):
    grad_x = derive(padded, 2)
    grad_y = derive(padded, 3)
    grad_z = derive(padded, 1)
    return jnp.stack(
        [
            grad_x[0] + grad_y[3] + grad_z[4],
            grad_x[3] + grad_y[1] + grad_z[5],
            grad_x[4] + grad_y[5] + grad_z[2],
        ]
    )


def pad_depth(field):
    return jnp.pad(field, ((0, 0), (2, 2), (0, 0), (0, 0)))


def shards(
    u_now,
    u_prev,
    lame_lambda,
    lame_mu,
    buoyancy,
    q_now,
    q_prev,
    archetype,
    stiffness,
    couple,
    counts,
    footprint,
):
    highest = lax.Precision.HIGHEST
    cells_x = u_now.shape[2]
    cells_y = u_now.shape[3]
    owners = lax.axis_size("gy")
    slots = q_now.shape[0]
    capacity = slots // owners
    home = lax.axis_index("gy")
    cells = footprint[0, 0]
    row_counts = lax.dynamic_index_in_dim(counts[0], home, 0, keepdims=False)
    active_slots = (
        (jnp.arange(capacity, dtype=jnp.int32)[None, :] < row_counts[:, None])
        .astype(jnp.float32)
        .reshape(slots)
    )
    kinds = stiffness.shape[0]
    onehot = (archetype[:, None] == jnp.arange(kinds, dtype=jnp.int32)[None, :]).astype(jnp.float32)
    stiff_table = stiffness.transpose(2, 0, 1).reshape(FRAME_FREEDOMS, kinds * FRAME_FREEDOMS)
    drive_table = couple.transpose(1, 0, 2).reshape(3, kinds * FRAME_FREEDOMS)
    shear_table = couple.transpose(2, 0, 1).reshape(FRAME_FREEDOMS, kinds * 3)
    field, older = (u_now, u_prev)
    frame_state, prior_frame_state = (q_now, q_prev)
    for counter in range(STEPS):
        surface = field[:, 0].reshape(3, cells_x * cells_y)
        base_layer = (
            surface[:, cells].reshape(3, slots, FOOTPRINT_CELLS).sum(axis=2)
            / FOOTPRINT_CELLS
            * active_slots
        )
        ground_motion = lax.all_to_all(base_layer, "gy", split_axis=1, concat_axis=1, tiled=True)
        shear_all = jnp.dot(frame_state, shear_table, precision=highest).reshape(slots, kinds, 3)
        shear_force = jnp.sum(shear_all * onehot[:, :, None], axis=1)
        returned = (
            lax.all_to_all(shear_force.T, "gy", split_axis=1, concat_axis=1, tiled=True)
            * active_slots
        )
        contrib = jnp.repeat(returned / FOOTPRINT_CELLS, FOOTPRINT_CELLS, axis=1)
        force = (
            jnp.zeros((3, cells_x * cells_y), jnp.float32)
            .at[:, cells]
            .add(contrib)
            .reshape(3, cells_x, cells_y)
        )
        rimmed = with_halo(field, (("gx", 2), ("gy", 3)), 2)
        inner = stress_of(pad_depth(rimmed), lame_lambda, lame_mu)
        stress = with_halo(inner, (("gx", 2), ("gy", 3)), 2)
        total = divergence(pad_depth(stress))
        total = total.at[:, 0].add(force)
        field_new = 2.0 * field - older + time_step * time_step * (buoyancy * total)
        stiff_all = jnp.dot(frame_state, stiff_table, precision=highest).reshape(
            slots, kinds, FRAME_FREEDOMS
        )
        stiff_term = jnp.sum(stiff_all * onehot[:, :, None], axis=1)
        drive_all = jnp.dot(ground_motion.T, drive_table, precision=highest).reshape(
            slots, kinds, FRAME_FREEDOMS
        )
        drive = jnp.sum(drive_all * onehot[:, :, None], axis=1)
        next_frame_state = (
            2.0 * frame_state - prior_frame_state + time_step * time_step * (drive - stiff_term)
        )
        older, field = (field, field_new)
        prior_frame_state, frame_state = (frame_state, next_frame_state)
    return (field, older, frame_state, prior_frame_state)


def solution(mesh):
    return jax.shard_map(
        shards,
        mesh=mesh,
        in_specs=(
            P(None, None, "gx", "gy"),
            P(None, None, "gx", "gy"),
            P(None, "gx", "gy"),
            P(None, "gx", "gy"),
            P(None, "gx", "gy"),
            P(("gx", "gy"), None),
            P(("gx", "gy"), None),
            P(("gx", "gy")),
            P(),
            P(),
            P("gx", None, None),
            P("gx", "gy", None),
        ),
        out_specs=(
            P(None, None, "gx", "gy"),
            P(None, None, "gx", "gy"),
            P(("gx", "gy"), None),
            P(("gx", "gy"), None),
        ),
        check_vma=False,
    )
```

profile of v0, /device:TPU:18, one launch (start us, length us, event | category | flops | bytes accessed | tf_op | source)
XLA Modules:
  0.0 116.6 jit_solution(14297653245160464524)
XLA Ops:
  0.7 1.0 fusion.106
  1.7 1.9 %collective-permute-start.1 = (f32[3,6,2,128]{3,2,1,0:T(2,128)S(1)}, f32[3,6,2,128]{3,2,1,0:T(2,128)S(1)}, u32[]{:S(2)}, u32[]{:S(2)}) collective-permute-start(f32[3,6,2,128]{3,2,1,0:T(2,128)S(1)} %get-tuple-element.55), channel_id=1, source_target_pairs={{0,4},{4,8},{8,12},{12,16},{16,20},{20,24},{24,28},{1,5},{5,9},{9,... | collective-permute-start | bytes 55304 | tf_op jit(solution)/shard_map/ppermute | solution.py:19
  3.6 3.6 %collective-permute-start = (f32[3,6,2,128]{3,2,1,0:T(2,128)S(1)}, f32[3,6,2,128]{3,2,1,0:T(2,128)S(1)}, u32[]{:S(2)}, u32[]{:S(2)}) collective-permute-start(f32[3,6,2,128]{3,2,1,0:T(2,128)S(1)} %get-tuple-element.54), channel_id=1, source_target_pairs={{4,0},{8,4},{12,8},{16,12},{20,16},{24,20},{28,24},{5,1},{9,5},{13... | collective-permute-start | bytes 55304 | tf_op jit(solution)/shard_map/ppermute | solution.py:20
  7.3 0.6 copy-done.12
  8.3 0.6 copy.42
  8.9 5.2 %all-to-all-start = ((f32[3,4,16]{2,0,1:T(4,128)}), f32[3,4,16]{2,0,1:T(4,128)S(1)}, u32[]{:S(2)}, u32[]{:S(2)}) async-start(f32[3,4,16]{2,0,1:T(4,128)} %copy.42), calls=%async_computation | async-start | bytes 16384 | tf_op jit(solution)/shard_map/all_to_all | solution.py:118
  14.1 0.7 fusion.98
  14.9 0.6 copy-done.11
  15.6 0.7 fusion.2
  16.6 3.4 %collective-permute-start.3 = (f32[3,6,12,2]{3,2,1,0:T(8,128)S(1)}, f32[3,6,12,2]{3,2,1,0:T(8,128)S(1)}, u32[]{:S(2)}, u32[]{:S(2)}) collective-permute-start(f32[3,6,12,2]{3,2,1,0:T(8,128)S(1)} %get-tuple-element.48), channel_id=1, source_target_pairs={{0,1},{1,2},{2,3},{4,5},{5,6},{6,7},{8,9},{9,10},{10,11},{12,13},{... | collective-permute-start | bytes 5192 | tf_op jit(solution)/shard_map/ppermute | solution.py:19
  20.0 2.5 %collective-permute-start.2 = (f32[3,6,12,2]{3,2,1,0:T(8,128)S(1)}, f32[3,6,12,2]{3,2,1,0:T(8,128)S(1)}, u32[]{:S(2)}, u32[]{:S(2)}) collective-permute-start(f32[3,6,12,2]{3,2,1,0:T(8,128)S(1)} %get-tuple-element.49), channel_id=1, source_target_pairs={{1,0},{2,1},{3,2},{5,4},{6,5},{7,6},{9,8},{10,9},{11,10},{13,12},{... | collective-permute-start | bytes 5192 | tf_op jit(solution)/shard_map/ppermute | solution.py:20
  22.5 0.6 slice-done
  23.4 0.7 gather_fusion
  24.4 2.6 %collective-permute-done.2 = f32[3,6,12,2]{3,2,1,0:T(8,128)S(1)} collective-permute-done((f32[3,6,12,2]{3,2,1,0:T(8,128)S(1)}, f32[3,6,12,2]{3,2,1,0:T(8,128)S(1)}, u32[]{:S(2)}, u32[]{:S(2)}) %collective-permute-start.2) | collective-permute-done | bytes 1760 | tf_op jit(solution)/shard_map/ppermute | solution.py:20
  28.5 1.9 %collective-permute-start.4 = (f32[6,6,2,128]{3,2,1,0:T(2,128)S(1)}, f32[6,6,2,128]{3,2,1,0:T(2,128)S(1)}, u32[]{:S(2)}, u32[]{:S(2)}) collective-permute-start(f32[6,6,2,128]{3,2,1,0:T(2,128)S(1)} %get-tuple-element.47), channel_id=1, source_target_pairs={{4,0},{8,4},{12,8},{16,12},{20,16},{24,20},{28,24},{5,1},{9,5},{13... | collective-permute-start | bytes 110600 | tf_op jit(solution)/shard_map/ppermute | solution.py:20
  30.4 2.4 %collective-permute-start.5 = (f32[6,6,2,128]{3,2,1,0:T(2,128)S(1)}, f32[6,6,2,128]{3,2,1,0:T(2,128)S(1)}, u32[]{:S(2)}, u32[]{:S(2)}) collective-permute-start(f32[6,6,2,128]{3,2,1,0:T(2,128)S(1)} %get-tuple-element.46), channel_id=1, source_target_pairs={{0,4},{4,8},{8,12},{12,16},{16,20},{20,24},{24,28},{1,5},{5,9},{9,... | collective-permute-start | bytes 110600 | tf_op jit(solution)/shard_map/ppermute | solution.py:19
  32.9 1.6 %scatter_custom_fusion = f32[3,1024]{0,1:T(8,128)S(1)} fusion(s32[256]{0:T(256)S(1)} %bitcast.205, f32[256,3]{1,0:T(8,128)S(1)} %bitcast.197, f32[]{:T(128)} %constant.90.clone.1), kind=kCustom, calls=%fused_computation.50 | custom fusion | flops 768 | bytes 12292 | tf_op jit(solution)/shard_map/scatter-add | solution.py:125
  34.7 1.0 collective-permute-done.5
  35.9 2.5 %collective-permute-start.6 = (f32[6,6,12,2]{3,2,1,0:T(8,128)S(1)}, f32[6,6,12,2]{3,2,1,0:T(8,128)S(1)}, u32[]{:S(2)}, u32[]{:S(2)}) collective-permute-start(f32[6,6,12,2]{3,2,1,0:T(8,128)S(1)} %get-tuple-element.41), channel_id=1, source_target_pairs={{1,0},{2,1},{3,2},{5,4},{6,5},{7,6},{9,8},{10,9},{11,10},{13,12},{... | collective-permute-start | bytes 10376 | tf_op jit(solution)/shard_map/ppermute | solution.py:20
  38.3 3.4 %collective-permute-start.7 = (f32[6,6,12,2]{3,2,1,0:T(8,128)S(1)}, f32[6,6,12,2]{3,2,1,0:T(8,128)S(1)}, u32[]{:S(2)}, u32[]{:S(2)}) collective-permute-start(f32[6,6,12,2]{3,2,1,0:T(8,128)S(1)} %get-tuple-element.40), channel_id=1, source_target_pairs={{0,1},{1,2},{2,3},{4,5},{5,6},{6,7},{8,9},{9,10},{10,11},{12,13},{... | collective-permute-start | bytes 10376 | tf_op jit(solution)/shard_map/ppermute | solution.py:19
  41.9 5.7 %collective-permute-done.6 = f32[6,6,12,2]{3,2,1,0:T(8,128)S(1)} collective-permute-done((f32[6,6,12,2]{3,2,1,0:T(8,128)S(1)}, f32[6,6,12,2]{3,2,1,0:T(8,128)S(1)}, u32[]{:S(2)}, u32[]{:S(2)}) %collective-permute-start.6) | collective-permute-done | bytes 3488 | tf_op jit(solution)/shard_map/ppermute | solution.py:20
  47.6 2.3 %collective-permute-done.7 = f32[6,6,12,2]{3,2,1,0:T(8,128)S(1)} collective-permute-done((f32[6,6,12,2]{3,2,1,0:T(8,128)S(1)}, f32[6,6,12,2]{3,2,1,0:T(8,128)S(1)}, u32[]{:S(2)}, u32[]{:S(2)}) %collective-permute-start.7) | collective-permute-done | bytes 3488 | tf_op jit(solution)/shard_map/ppermute | solution.py:19
  51.2 0.8 copy-done.8
  52.3 0.7 gather_fusion.1
  53.2 0.6 broadcast_multiply_fusion
  53.8 5.1 %all-to-all-start.1 = ((f32[3,4,16]{2,0,1:T(4,128)}), f32[3,4,16]{2,0,1:T(4,128)S(1)}, u32[]{:S(2)}, u32[]{:S(2)}) async-start(f32[3,4,16]{2,0,1:T(4,128)} %get-tuple-element.57), calls=%async_computation.1 | async-start | bytes 16384 | tf_op jit(solution)/shard_map/all_to_all | solution.py:114
  58.9 1.9 %collective-permute-start.9 = (f32[3,6,2,128]{3,2,1,0:T(2,128)S(1)}, f32[3,6,2,128]{3,2,1,0:T(2,128)S(1)}, u32[]{:S(2)}, u32[]{:S(2)}) collective-permute-start(f32[3,6,2,128]{3,2,1,0:T(2,128)S(1)} %get-tuple-element.51), channel_id=1, source_target_pairs={{0,4},{4,8},{8,12},{12,16},{16,20},{20,24},{24,28},{1,5},{5,9},{9,... | collective-permute-start | bytes 55304 | tf_op jit(solution)/shard_map/ppermute | solution.py:19
  60.9 3.6 %collective-permute-start.8 = (f32[3,6,2,128]{3,2,1,0:T(2,128)S(1)}, f32[3,6,2,128]{3,2,1,0:T(2,128)S(1)}, u32[]{:S(2)}, u32[]{:S(2)}) collective-permute-start(f32[3,6,2,128]{3,2,1,0:T(2,128)S(1)} %get-tuple-element.50), channel_id=1, source_target_pairs={{4,0},{8,4},{12,8},{16,12},{20,16},{24,20},{28,24},{5,1},{9,5},{13... | collective-permute-start | bytes 55304 | tf_op jit(solution)/shard_map/ppermute | solution.py:20
  64.5 5.1 %all-to-all-start.3 = ((f32[3,4,16]{2,0,1:T(4,128)}), f32[3,4,16]{2,0,1:T(4,128)S(1)}, u32[]{:S(2)}, u32[]{:S(2)}) async-start(f32[3,4,16]{2,0,1:T(4,128)} %get-tuple-element.56), calls=%async_computation.3 | async-start | bytes 16384 | tf_op jit(solution)/shard_map/all_to_all | solution.py:114
  70.5 0.7 fusion.3
  71.5 0.6 copy.50
  72.1 0.8 all-to-all-done.3
  72.9 5.6 %all-to-all-start.2 = ((f32[3,4,16]{2,0,1:T(4,128)}), f32[3,4,16]{2,0,1:T(4,128)S(1)}, u32[]{:S(2)}, u32[]{:S(2)}) async-start(f32[3,4,16]{2,0,1:T(4,128)} %copy.50), calls=%async_computation.2 | async-start | bytes 16384 | tf_op jit(solution)/shard_map/all_to_all | solution.py:118
  79.0 0.6 multiply_add_fusion.2
  79.6 2.1 %all-to-all-done.2 = f32[3,4,16]{2,0,1:T(4,128)S(1)} async-done(((f32[3,4,16]{2,0,1:T(4,128)}), f32[3,4,16]{2,0,1:T(4,128)S(1)}, u32[]{:S(2)}, u32[]{:S(2)}) %all-to-all-start.2) | async-done | bytes 800 | tf_op jit(solution)/shard_map/all_to_all | solution.py:118
  81.9 3.4 %collective-permute-start.10 = (f32[3,6,12,2]{3,2,1,0:T(8,128)S(1)}, f32[3,6,12,2]{3,2,1,0:T(8,128)S(1)}, u32[]{:S(2)}, u32[]{:S(2)}) collective-permute-start(f32[3,6,12,2]{3,2,1,0:T(8,128)S(1)} %get-tuple-element.45), channel_id=1, source_target_pairs={{1,0},{2,1},{3,2},{5,4},{6,5},{7,6},{9,8},{10,9},{11,10},{13,12},{... | collective-permute-start | bytes 5192 | tf_op jit(solution)/shard_map/ppermute | solution.py:20
  85.3 2.5 %collective-permute-start.11 = (f32[3,6,12,2]{3,2,1,0:T(8,128)S(1)}, f32[3,6,12,2]{3,2,1,0:T(8,128)S(1)}, u32[]{:S(2)}, u32[]{:S(2)}) collective-permute-start(f32[3,6,12,2]{3,2,1,0:T(8,128)S(1)} %get-tuple-element.44), channel_id=1, source_target_pairs={{0,1},{1,2},{2,3},{4,5},{5,6},{6,7},{8,9},{9,10},{10,11},{12,13},{... | collective-permute-start | bytes 5192 | tf_op jit(solution)/shard_map/ppermute | solution.py:19
  87.9 1.1 collective-permute-done.10
  89.0 3.4 %collective-permute-done.11 = f32[3,6,12,2]{3,2,1,0:T(8,128)S(1)} collective-permute-done((f32[3,6,12,2]{3,2,1,0:T(8,128)S(1)}, f32[3,6,12,2]{3,2,1,0:T(8,128)S(1)}, u32[]{:S(2)}, u32[]{:S(2)}) %collective-permute-start.11) | collective-permute-done | bytes 1760 | tf_op jit(solution)/shard_map/ppermute | solution.py:19
  93.2 1.9 %collective-permute-start.12 = (f32[6,6,2,128]{3,2,1,0:T(2,128)S(1)}, f32[6,6,2,128]{3,2,1,0:T(2,128)S(1)}, u32[]{:S(2)}, u32[]{:S(2)}) collective-permute-start(f32[6,6,2,128]{3,2,1,0:T(2,128)S(1)} %get-tuple-element.43), channel_id=1, source_target_pairs={{4,0},{8,4},{12,8},{16,12},{20,16},{24,20},{28,24},{5,1},{9,5},{13... | collective-permute-start | bytes 110600 | tf_op jit(solution)/shard_map/ppermute | solution.py:20
  95.2 2.4 %collective-permute-start.13 = (f32[6,6,2,128]{3,2,1,0:T(2,128)S(1)}, f32[6,6,2,128]{3,2,1,0:T(2,128)S(1)}, u32[]{:S(2)}, u32[]{:S(2)}) collective-permute-start(f32[6,6,2,128]{3,2,1,0:T(2,128)S(1)} %get-tuple-element.42), channel_id=1, source_target_pairs={{0,4},{4,8},{8,12},{12,16},{16,20},{20,24},{24,28},{1,5},{5,9},{9,... | collective-permute-start | bytes 110600 | tf_op jit(solution)/shard_map/ppermute | solution.py:19
  97.7 1.6 %scatter_custom_fusion.1 = f32[3,1024]{0,1:T(8,128)S(1)} fusion(s32[256]{0:T(256)S(1)} %bitcast.206, f32[256,3]{1,0:T(8,128)S(1)} %bitcast.196, f32[]{:T(128)} %constant.90.clone.1), kind=kCustom, calls=%fused_computation.48 | custom fusion | flops 768 | bytes 12292 | tf_op jit(solution)/shard_map/scatter-add | solution.py:125
  99.5 1.0 collective-permute-done.13
  100.6 3.3 %collective-permute-start.14 = (f32[6,6,12,2]{3,2,1,0:T(8,128)S(1)}, f32[6,6,12,2]{3,2,1,0:T(8,128)S(1)}, u32[]{:S(2)}, u32[]{:S(2)}) collective-permute-start(f32[6,6,12,2]{3,2,1,0:T(8,128)S(1)} %get-tuple-element.39), channel_id=1, source_target_pairs={{1,0},{2,1},{3,2},{5,4},{6,5},{7,6},{9,8},{10,9},{11,10},{13,12},{... | collective-permute-start | bytes 10376 | tf_op jit(solution)/shard_map/ppermute | solution.py:20
  104.0 2.5 %collective-permute-start.15 = (f32[6,6,12,2]{3,2,1,0:T(8,128)S(1)}, f32[6,6,12,2]{3,2,1,0:T(8,128)S(1)}, u32[]{:S(2)}, u32[]{:S(2)}) collective-permute-start(f32[6,6,12,2]{3,2,1,0:T(8,128)S(1)} %get-tuple-element.38), channel_id=1, source_target_pairs={{0,1},{1,2},{2,3},{4,5},{5,6},{6,7},{8,9},{9,10},{10,11},{12,13},{... | collective-permute-start | bytes 10376 | tf_op jit(solution)/shard_map/ppermute | solution.py:19
  106.6 4.9 %collective-permute-done.14 = f32[6,6,12,2]{3,2,1,0:T(8,128)S(1)} collective-permute-done((f32[6,6,12,2]{3,2,1,0:T(8,128)S(1)}, f32[6,6,12,2]{3,2,1,0:T(8,128)S(1)}, u32[]{:S(2)}, u32[]{:S(2)}) %collective-permute-start.14) | collective-permute-done | bytes 3488 | tf_op jit(solution)/shard_map/ppermute | solution.py:20
  111.6 3.1 %collective-permute-done.15 = f32[6,6,12,2]{3,2,1,0:T(8,128)S(1)} collective-permute-done((f32[6,6,12,2]{3,2,1,0:T(8,128)S(1)}, f32[6,6,12,2]{3,2,1,0:T(8,128)S(1)}, u32[]{:S(2)}, u32[]{:S(2)}) %collective-permute-start.15) | collective-permute-done | bytes 3488 | tf_op jit(solution)/shard_map/ppermute | solution.py:19
  115.9 0.7 multiply_add_fusion
  (118 shorter events, 9.7 us)
Async XLA Ops:
  0.6 14.9 %copy-start = (f32[8,128,128]{2,1,0:T(8,128)S(1)}, f32[8,128,128]{2,1,0:T(8,128)}, u32[]{:S(2)}) copy-start(f32[8,128,128]{2,1,0:T(8,128)} %param.24) | copy-start | bytes 1572868
  0.6 6.6 %copy-start.10 = (f32[8,3,128]{2,0,1:T(8,128)S(1)}, f32[8,3,128]{2,0,1:T(8,128)}, u32[]{:S(2)}) copy-start(f32[8,3,128]{2,0,1:T(8,128)} %param.25) | copy-start | bytes 36868
  1.7 14.6 %collective-permute-start.1 = (f32[3,6,2,128]{3,2,1,0:T(2,128)S(1)}, f32[3,6,2,128]{3,2,1,0:T(2,128)S(1)}, u32[]{:S(2)}, u32[]{:S(2)}) collective-permute-start(f32[3,6,2,128]{3,2,1,0:T(2,128)S(1)} %get-tuple-element.55), channel_id=1, source_target_pairs={{0,4},{4,8},{8,12},{12,16},{16,20},{20,24},{24,28},{1,5},{5,9},{9,... | collective-permute-start | bytes 55304 | tf_op jit(solution)/shard_map/ppermute | solution.py:19
  3.6 12.7 %collective-permute-start = (f32[3,6,2,128]{3,2,1,0:T(2,128)S(1)}, f32[3,6,2,128]{3,2,1,0:T(2,128)S(1)}, u32[]{:S(2)}, u32[]{:S(2)}) collective-permute-start(f32[3,6,2,128]{3,2,1,0:T(2,128)S(1)} %get-tuple-element.54), channel_id=1, source_target_pairs={{4,0},{8,4},{12,8},{16,12},{20,16},{24,20},{28,24},{5,1},{9,5},{13... | collective-permute-start | bytes 55304 | tf_op jit(solution)/shard_map/ppermute | solution.py:20
  7.3 0.8 copy-start.4
  7.3 0.7 copy-start.12
  8.9 15.4 %all-to-all-start = ((f32[3,4,16]{2,0,1:T(4,128)}), f32[3,4,16]{2,0,1:T(4,128)S(1)}, u32[]{:S(2)}, u32[]{:S(2)}) async-start(f32[3,4,16]{2,0,1:T(4,128)} %copy.42), calls=%async_computation | async-start | bytes 16384 | tf_op jit(solution)/shard_map/all_to_all | solution.py:118
  14.9 0.7 copy-start.11
  15.6 0.9 copy-start.2
  16.6 7.8 %collective-permute-start.3 = (f32[3,6,12,2]{3,2,1,0:T(8,128)S(1)}, f32[3,6,12,2]{3,2,1,0:T(8,128)S(1)}, u32[]{:S(2)}, u32[]{:S(2)}) collective-permute-start(f32[3,6,12,2]{3,2,1,0:T(8,128)S(1)} %get-tuple-element.48), channel_id=1, source_target_pairs={{0,1},{1,2},{2,3},{4,5},{5,6},{6,7},{8,9},{9,10},{10,11},{12,13},{... | collective-permute-start | bytes 5192 | tf_op jit(solution)/shard_map/ppermute | solution.py:19
  20.0 7.0 %collective-permute-start.2 = (f32[3,6,12,2]{3,2,1,0:T(8,128)S(1)}, f32[3,6,12,2]{3,2,1,0:T(8,128)S(1)}, u32[]{:S(2)}, u32[]{:S(2)}) collective-permute-start(f32[3,6,12,2]{3,2,1,0:T(8,128)S(1)} %get-tuple-element.49), channel_id=1, source_target_pairs={{1,0},{2,1},{3,2},{5,4},{6,5},{7,6},{9,8},{10,9},{11,10},{13,12},{... | collective-permute-start | bytes 5192 | tf_op jit(solution)/shard_map/ppermute | solution.py:20
  22.4 0.7 slice-start
  27.6 0.7 copy-start.1
  27.6 0.7 copy-start.7
  28.5 6.2 %collective-permute-start.4 = (f32[6,6,2,128]{3,2,1,0:T(2,128)S(1)}, f32[6,6,2,128]{3,2,1,0:T(2,128)S(1)}, u32[]{:S(2)}, u32[]{:S(2)}) collective-permute-start(f32[6,6,2,128]{3,2,1,0:T(2,128)S(1)} %get-tuple-element.47), channel_id=1, source_target_pairs={{4,0},{8,4},{12,8},{16,12},{20,16},{24,20},{28,24},{5,1},{9,5},{13... | collective-permute-start | bytes 110600 | tf_op jit(solution)/shard_map/ppermute | solution.py:20
  30.4 5.3 %collective-permute-start.5 = (f32[6,6,2,128]{3,2,1,0:T(2,128)S(1)}, f32[6,6,2,128]{3,2,1,0:T(2,128)S(1)}, u32[]{:S(2)}, u32[]{:S(2)}) collective-permute-start(f32[6,6,2,128]{3,2,1,0:T(2,128)S(1)} %get-tuple-element.46), channel_id=1, source_target_pairs={{0,4},{4,8},{8,12},{12,16},{16,20},{20,24},{24,28},{1,5},{5,9},{9,... | collective-permute-start | bytes 110600 | tf_op jit(solution)/shard_map/ppermute | solution.py:19
  35.9 11.7 %collective-permute-start.6 = (f32[6,6,12,2]{3,2,1,0:T(8,128)S(1)}, f32[6,6,12,2]{3,2,1,0:T(8,128)S(1)}, u32[]{:S(2)}, u32[]{:S(2)}) collective-permute-start(f32[6,6,12,2]{3,2,1,0:T(8,128)S(1)} %get-tuple-element.41), channel_id=1, source_target_pairs={{1,0},{2,1},{3,2},{5,4},{6,5},{7,6},{9,8},{10,9},{11,10},{13,12},{... | collective-permute-start | bytes 10376 | tf_op jit(solution)/shard_map/ppermute | solution.py:20
  38.3 11.6 %collective-permute-start.7 = (f32[6,6,12,2]{3,2,1,0:T(8,128)S(1)}, f32[6,6,12,2]{3,2,1,0:T(8,128)S(1)}, u32[]{:S(2)}, u32[]{:S(2)}) collective-permute-start(f32[6,6,12,2]{3,2,1,0:T(8,128)S(1)} %get-tuple-element.40), channel_id=1, source_target_pairs={{0,1},{1,2},{2,3},{4,5},{5,6},{6,7},{8,9},{9,10},{10,11},{12,13},{... | collective-permute-start | bytes 10376 | tf_op jit(solution)/shard_map/ppermute | solution.py:19
  51.1 0.9 copy-start.8
  51.2 0.9 copy-start.6
  52.0 63.9 %copy-start.3 = (f32[3,6,8,128]{3,2,1,0:T(8,128)}, f32[3,6,8,128]{3,2,1,0:T(8,128)S(1)}, u32[]{:S(2)}) copy-start(f32[3,6,8,128]{3,2,1,0:T(8,128)S(1)} %multiply_add_fusion.1) | copy-start | bytes 221188
  53.8 10.7 %all-to-all-start.1 = ((f32[3,4,16]{2,0,1:T(4,128)}), f32[3,4,16]{2,0,1:T(4,128)S(1)}, u32[]{:S(2)}, u32[]{:S(2)}) async-start(f32[3,4,16]{2,0,1:T(4,128)} %get-tuple-element.57), calls=%async_computation.1 | async-start | bytes 16384 | tf_op jit(solution)/shard_map/all_to_all | solution.py:114
  58.9 22.9 %collective-permute-start.9 = (f32[3,6,2,128]{3,2,1,0:T(2,128)S(1)}, f32[3,6,2,128]{3,2,1,0:T(2,128)S(1)}, u32[]{:S(2)}, u32[]{:S(2)}) collective-permute-start(f32[3,6,2,128]{3,2,1,0:T(2,128)S(1)} %get-tuple-element.51), channel_id=1, source_target_pairs={{0,4},{4,8},{8,12},{12,16},{16,20},{20,24},{24,28},{1,5},{5,9},{9,... | collective-permute-start | bytes 55304 | tf_op jit(solution)/shard_map/ppermute | solution.py:19
  60.9 20.9 %collective-permute-start.8 = (f32[3,6,2,128]{3,2,1,0:T(2,128)S(1)}, f32[3,6,2,128]{3,2,1,0:T(2,128)S(1)}, u32[]{:S(2)}, u32[]{:S(2)}) collective-permute-start(f32[3,6,2,128]{3,2,1,0:T(2,128)S(1)} %get-tuple-element.50), channel_id=1, source_target_pairs={{4,0},{8,4},{12,8},{16,12},{20,16},{24,20},{28,24},{5,1},{9,5},{13... | collective-permute-start | bytes 55304 | tf_op jit(solution)/shard_map/ppermute | solution.py:20
  64.5 8.4 %all-to-all-start.3 = ((f32[3,4,16]{2,0,1:T(4,128)}), f32[3,4,16]{2,0,1:T(4,128)S(1)}, u32[]{:S(2)}, u32[]{:S(2)}) async-start(f32[3,4,16]{2,0,1:T(4,128)} %get-tuple-element.56), calls=%async_computation.3 | async-start | bytes 16384 | tf_op jit(solution)/shard_map/all_to_all | solution.py:114
  69.7 0.8 copy-start.9
  70.5 8.5 %copy-start.5 = (f32[64,128]{1,0:T(8,128)}, f32[64,128]{1,0:T(8,128)S(1)}, u32[]{:S(2)}) copy-start(f32[64,128]{1,0:T(8,128)S(1)} %multiply_add_fusion.3) | copy-start | bytes 98308
  72.9 8.8 %all-to-all-start.2 = ((f32[3,4,16]{2,0,1:T(4,128)}), f32[3,4,16]{2,0,1:T(4,128)S(1)}, u32[]{:S(2)}, u32[]{:S(2)}) async-start(f32[3,4,16]{2,0,1:T(4,128)} %copy.50), calls=%async_computation.2 | async-start | bytes 16384 | tf_op jit(solution)/shard_map/all_to_all | solution.py:118
  81.9 7.0 %collective-permute-start.10 = (f32[3,6,12,2]{3,2,1,0:T(8,128)S(1)}, f32[3,6,12,2]{3,2,1,0:T(8,128)S(1)}, u32[]{:S(2)}, u32[]{:S(2)}) collective-permute-start(f32[3,6,12,2]{3,2,1,0:T(8,128)S(1)} %get-tuple-element.45), channel_id=1, source_target_pairs={{1,0},{2,1},{3,2},{5,4},{6,5},{7,6},{9,8},{10,9},{11,10},{13,12},{... | collective-permute-start | bytes 5192 | tf_op jit(solution)/shard_map/ppermute | solution.py:20
  85.3 7.0 %collective-permute-start.11 = (f32[3,6,12,2]{3,2,1,0:T(8,128)S(1)}, f32[3,6,12,2]{3,2,1,0:T(8,128)S(1)}, u32[]{:S(2)}, u32[]{:S(2)}) collective-permute-start(f32[3,6,12,2]{3,2,1,0:T(8,128)S(1)} %get-tuple-element.44), channel_id=1, source_target_pairs={{0,1},{1,2},{2,3},{4,5},{5,6},{6,7},{8,9},{9,10},{10,11},{12,13},{... | collective-permute-start | bytes 5192 | tf_op jit(solution)/shard_map/ppermute | solution.py:19
  93.2 6.2 %collective-permute-start.12 = (f32[6,6,2,128]{3,2,1,0:T(2,128)S(1)}, f32[6,6,2,128]{3,2,1,0:T(2,128)S(1)}, u32[]{:S(2)}, u32[]{:S(2)}) collective-permute-start(f32[6,6,2,128]{3,2,1,0:T(2,128)S(1)} %get-tuple-element.43), channel_id=1, source_target_pairs={{4,0},{8,4},{12,8},{16,12},{20,16},{24,20},{28,24},{5,1},{9,5},{13... | collective-permute-start | bytes 110600 | tf_op jit(solution)/shard_map/ppermute | solution.py:20
  95.2 5.3 %collective-permute-start.13 = (f32[6,6,2,128]{3,2,1,0:T(2,128)S(1)}, f32[6,6,2,128]{3,2,1,0:T(2,128)S(1)}, u32[]{:S(2)}, u32[]{:S(2)}) collective-permute-start(f32[6,6,2,128]{3,2,1,0:T(2,128)S(1)} %get-tuple-element.42), channel_id=1, source_target_pairs={{0,4},{4,8},{8,12},{12,16},{16,20},{20,24},{24,28},{1,5},{5,9},{9,... | collective-permute-start | bytes 110600 | tf_op jit(solution)/shard_map/ppermute | solution.py:19
  100.6 11.0 %collective-permute-start.14 = (f32[6,6,12,2]{3,2,1,0:T(8,128)S(1)}, f32[6,6,12,2]{3,2,1,0:T(8,128)S(1)}, u32[]{:S(2)}, u32[]{:S(2)}) collective-permute-start(f32[6,6,12,2]{3,2,1,0:T(8,128)S(1)} %get-tuple-element.39), channel_id=1, source_target_pairs={{1,0},{2,1},{3,2},{5,4},{6,5},{7,6},{9,8},{10,9},{11,10},{13,12},{... | collective-permute-start | bytes 10376 | tf_op jit(solution)/shard_map/ppermute | solution.py:20
  104.0 10.7 %collective-permute-start.15 = (f32[6,6,12,2]{3,2,1,0:T(8,128)S(1)}, f32[6,6,12,2]{3,2,1,0:T(8,128)S(1)}, u32[]{:S(2)}, u32[]{:S(2)}) collective-permute-start(f32[6,6,12,2]{3,2,1,0:T(8,128)S(1)} %get-tuple-element.38), channel_id=1, source_target_pairs={{0,1},{1,2},{2,3},{4,5},{5,6},{6,7},{8,9},{9,10},{10,11},{12,13},{... | collective-permute-start | bytes 10376 | tf_op jit(solution)/shard_map/ppermute | solution.py:19
where the time goes:
time: 118 us; the launch traced here: 117 us
  starting transfers between devices  64.1 us (54%)
  waiting for transfers between devices  28 us (24%)
  local copies, waits for them, and re-layouts  10.7 us (9%)
  other arithmetic  9.77 us (8%)
  matrix products  2.55 us (2%)
  between operations  1.33 us (1%)
    ppermute x8, starting transfers between devices, with_halo(): after = lax.ppermute(initial, axis, down)  22.8 us
    ppermute x8, starting transfers between devices, with_halo(): before = lax.ppermute(last, axis, up)  20.4 us
    ppermute x8, waiting for transfers between devices, with_halo(): after = lax.ppermute(initial, axis, down)  14.3 us
    ppermute x8, waiting for transfers between devices, with_halo(): before = lax.ppermute(last, axis, up)  10.8 us
    all_to_all x2, starting transfers between devices, shards(): lax.all_to_all(shear_force.T, 'gy', split_axis=1, concat_axis=1, tiled=True)  10.8 us
    all_to_all x2, starting transfers between devices, shards(): lax.all_to_all(base_layer, 'gy', split_axis=1, concat_axis=1, tiled=True)  10.2 us
    unnamed x26, local copies, waits for them, and re-layouts  3.3 us
    scatter-add x2, other arithmetic, shards(): force = jnp.zeros((3, cells_x * cells_y), jnp.float32).at[:, cells].add(c...  3.1 us
  transfers between devices with their start and end apart: 20, of which 11 were waited for; matrix products, arithmetic and copies ran while one was open for 9% of the time, Pallas kernels for 0%

commit v1 on v0

--- a/solution.py
+++ b/solution.py
@@ -115,7 +115,12 @@
         shear_all = jnp.dot(frame_state, shear_table, precision=highest).reshape(slots, kinds, 3)
         shear_force = jnp.sum(shear_all * onehot[:, :, None], axis=1)
         returned = (
-            lax.all_to_all(shear_force.T, "gy", split_axis=1, concat_axis=1, tiled=True)
+            jnp.concatenate(
+                lax.all_to_all(
+                    jnp.stack(jnp.split(shear_force.T, lax.axis_size("gy"), axis=1)), "gy", 0, 0
+                ),
+                axis=1,
+            )
             * active_slots
         )
         contrib = jnp.repeat(returned / FOOTPRINT_CELLS, FOOTPRINT_CELLS, axis=1)

time: 118 us -> 118 us (level)
  other arithmetic: 9.77 us -> 11 us
  local copies, waits for them, and re-layouts: 10.7 us -> 9.47 us
    all_to_all x8 -> x0, local copies, waits for them, and re-layouts: 1.57 us -> none  [shards(): lax.all_to_all(shear_force.T, 'gy', split_axis=1, concat_axis=1, tiled=True)]
    another operation x0 -> x2, other arithmetic: none -> 1.22 us  [shards(): jnp.stack(jnp.split(shear_force.T, lax.axis_size('gy'), axis=1))]
  transfers between devices with their start and end apart: 20 -> 20, of which waited for: 11 -> 11; matrix products, arithmetic and copies ran while one was open for 9% -> 10% of each run, Pallas kernels for 0% -> 0%
where the time goes in v1:
time: 118 us; the launch traced here: 117 us
  starting transfers between devices  64.1 us (54%)
  waiting for transfers between devices  28.1 us (24%)
  other arithmetic  11 us (9%)
  local copies, waits for them, and re-layouts  9.47 us (8%)
  matrix products  2.55 us (2%)
  between operations  1.33 us (1%)
    ppermute x8, starting transfers between devices, with_halo(): after = lax.ppermute(initial, axis, down)  22.8 us
    ppermute x8, starting transfers between devices, with_halo(): before = lax.ppermute(last, axis, up)  20.4 us
    ppermute x8, waiting for transfers between devices, with_halo(): after = lax.ppermute(initial, axis, down)  14.3 us
    ppermute x8, waiting for transfers between devices, with_halo(): before = lax.ppermute(last, axis, up)  10.8 us
    all_to_all x2, starting transfers between devices, shards(): lax.all_to_all(jnp.stack(jnp.split(shear_force.T, lax.axis_size('gy'), ax...  10.8 us
    all_to_all x2, starting transfers between devices, shards(): lax.all_to_all(base_layer, 'gy', split_axis=1, concat_axis=1, tiled=True)  10.2 us
    unnamed x26, local copies, waits for them, and re-layouts  3.3 us
    scatter-add x2, other arithmetic, shards(): force = jnp.zeros((3, cells_x * cells_y), jnp.float32).at[:, cells].add(c...  3.1 us
  transfers between devices with their start and end apart: 20, of which 11 were waited for; matrix products, arithmetic and copies ran while one was open for 10% of the time, Pallas kernels for 0%

profile of v1, /device:TPU:18, one launch (start us, length us, event | category | flops | bytes accessed | tf_op | source)
XLA Modules:
  0.0 116.6 jit_solution(2574577545395764249)
XLA Ops:
  0.7 1.0 fusion.106
  1.7 1.9 %collective-permute-start.1 = (f32[3,6,2,128]{3,2,1,0:T(2,128)S(1)}, f32[3,6,2,128]{3,2,1,0:T(2,128)S(1)}, u32[]{:S(2)}, u32[]{:S(2)}) collective-permute-start(f32[3,6,2,128]{3,2,1,0:T(2,128)S(1)} %get-tuple-element.55), channel_id=1, source_target_pairs={{0,4},{4,8},{8,12},{12,16},{16,20},{20,24},{24,28},{1,5},{5,9},{9,... | collective-permute-start | bytes 55304 | tf_op jit(solution)/shard_map/ppermute | solution.py:19
  3.6 3.6 %collective-permute-start = (f32[3,6,2,128]{3,2,1,0:T(2,128)S(1)}, f32[3,6,2,128]{3,2,1,0:T(2,128)S(1)}, u32[]{:S(2)}, u32[]{:S(2)}) collective-permute-start(f32[3,6,2,128]{3,2,1,0:T(2,128)S(1)} %get-tuple-element.54), channel_id=1, source_target_pairs={{4,0},{8,4},{12,8},{16,12},{20,16},{24,20},{28,24},{5,1},{9,5},{13... | collective-permute-start | bytes 55304 | tf_op jit(solution)/shard_map/ppermute | solution.py:20
  7.3 0.6 copy-done.12
  8.3 0.6 pad_maximum_fusion.37
  8.9 5.2 %all-to-all-start = ((f32[4,3,16]{2,1,0:T(4,128)}), f32[4,3,16]{2,1,0:T(4,128)S(1)}, u32[]{:S(2)}, u32[]{:S(2)}) async-start(f32[4,3,16]{2,1,0:T(4,128)} %pad_maximum_fusion.37), calls=%async_computation | async-start | bytes 16384 | tf_op jit(solution)/shard_map/all_to_all | solution.py:119
  14.1 0.7 fusion.98
  14.9 0.6 copy-done.11
  15.5 0.7 fusion.2
  16.6 3.4 %collective-permute-start.3 = (f32[3,6,12,2]{3,2,1,0:T(8,128)S(1)}, f32[3,6,12,2]{3,2,1,0:T(8,128)S(1)}, u32[]{:S(2)}, u32[]{:S(2)}) collective-permute-start(f32[3,6,12,2]{3,2,1,0:T(8,128)S(1)} %get-tuple-element.48), channel_id=1, source_target_pairs={{0,1},{1,2},{2,3},{4,5},{5,6},{6,7},{8,9},{9,10},{10,11},{12,13},{... | collective-permute-start | bytes 5192 | tf_op jit(solution)/shard_map/ppermute | solution.py:19
  19.9 2.5 %collective-permute-start.2 = (f32[3,6,12,2]{3,2,1,0:T(8,128)S(1)}, f32[3,6,12,2]{3,2,1,0:T(8,128)S(1)}, u32[]{:S(2)}, u32[]{:S(2)}) collective-permute-start(f32[3,6,12,2]{3,2,1,0:T(8,128)S(1)} %get-tuple-element.49), channel_id=1, source_target_pairs={{1,0},{2,1},{3,2},{5,4},{6,5},{7,6},{9,8},{10,9},{11,10},{13,12},{... | collective-permute-start | bytes 5192 | tf_op jit(solution)/shard_map/ppermute | solution.py:20
  22.5 0.6 slice-done
  23.4 0.7 gather_fusion
  24.4 2.6 %collective-permute-done.2 = f32[3,6,12,2]{3,2,1,0:T(8,128)S(1)} collective-permute-done((f32[3,6,12,2]{3,2,1,0:T(8,128)S(1)}, f32[3,6,12,2]{3,2,1,0:T(8,128)S(1)}, u32[]{:S(2)}, u32[]{:S(2)}) %collective-permute-start.2) | collective-permute-done | bytes 1760 | tf_op jit(solution)/shard_map/ppermute | solution.py:20
  28.4 1.9 %collective-permute-start.4 = (f32[6,6,2,128]{3,2,1,0:T(2,128)S(1)}, f32[6,6,2,128]{3,2,1,0:T(2,128)S(1)}, u32[]{:S(2)}, u32[]{:S(2)}) collective-permute-start(f32[6,6,2,128]{3,2,1,0:T(2,128)S(1)} %get-tuple-element.47), channel_id=1, source_target_pairs={{4,0},{8,4},{12,8},{16,12},{20,16},{24,20},{28,24},{5,1},{9,5},{13... | collective-permute-start | bytes 110600 | tf_op jit(solution)/shard_map/ppermute | solution.py:20
  30.4 2.4 %collective-permute-start.5 = (f32[6,6,2,128]{3,2,1,0:T(2,128)S(1)}, f32[6,6,2,128]{3,2,1,0:T(2,128)S(1)}, u32[]{:S(2)}, u32[]{:S(2)}) collective-permute-start(f32[6,6,2,128]{3,2,1,0:T(2,128)S(1)} %get-tuple-element.46), channel_id=1, source_target_pairs={{0,4},{4,8},{8,12},{12,16},{16,20},{20,24},{24,28},{1,5},{5,9},{9,... | collective-permute-start | bytes 110600 | tf_op jit(solution)/shard_map/ppermute | solution.py:19
  32.9 1.6 %scatter_custom_fusion = f32[3,1024]{0,1:T(8,128)S(1)} fusion(s32[256]{0:T(256)S(1)} %bitcast.225, f32[256,3]{1,0:T(8,128)S(1)} %bitcast.215, f32[]{:T(128)} %constant.90.clone.1), kind=kCustom, calls=%fused_computation.50 | custom fusion | flops 768 | bytes 12292 | tf_op jit(solution)/shard_map/scatter-add | solution.py:130
  34.7 1.0 collective-permute-done.5
  35.9 2.5 %collective-permute-start.6 = (f32[6,6,12,2]{3,2,1,0:T(8,128)S(1)}, f32[6,6,12,2]{3,2,1,0:T(8,128)S(1)}, u32[]{:S(2)}, u32[]{:S(2)}) collective-permute-start(f32[6,6,12,2]{3,2,1,0:T(8,128)S(1)} %get-tuple-element.41), channel_id=1, source_target_pairs={{1,0},{2,1},{3,2},{5,4},{6,5},{7,6},{9,8},{10,9},{11,10},{13,12},{... | collective-permute-start | bytes 10376 | tf_op jit(solution)/shard_map/ppermute | solution.py:20
  38.3 3.4 %collective-permute-start.7 = (f32[6,6,12,2]{3,2,1,0:T(8,128)S(1)}, f32[6,6,12,2]{3,2,1,0:T(8,128)S(1)}, u32[]{:S(2)}, u32[]{:S(2)}) collective-permute-start(f32[6,6,12,2]{3,2,1,0:T(8,128)S(1)} %get-tuple-element.40), channel_id=1, source_target_pairs={{0,1},{1,2},{2,3},{4,5},{5,6},{6,7},{8,9},{9,10},{10,11},{12,13},{... | collective-permute-start | bytes 10376 | tf_op jit(solution)/shard_map/ppermute | solution.py:19
  41.9 5.7 %collective-permute-done.6 = f32[6,6,12,2]{3,2,1,0:T(8,128)S(1)} collective-permute-done((f32[6,6,12,2]{3,2,1,0:T(8,128)S(1)}, f32[6,6,12,2]{3,2,1,0:T(8,128)S(1)}, u32[]{:S(2)}, u32[]{:S(2)}) %collective-permute-start.6) | collective-permute-done | bytes 3488 | tf_op jit(solution)/shard_map/ppermute | solution.py:20
  47.6 2.3 %collective-permute-done.7 = f32[6,6,12,2]{3,2,1,0:T(8,128)S(1)} collective-permute-done((f32[6,6,12,2]{3,2,1,0:T(8,128)S(1)}, f32[6,6,12,2]{3,2,1,0:T(8,128)S(1)}, u32[]{:S(2)}, u32[]{:S(2)}) %collective-permute-start.7) | collective-permute-done | bytes 3488 | tf_op jit(solution)/shard_map/ppermute | solution.py:19
  51.2 0.8 copy-done.8
  52.3 0.7 gather_fusion.1
  53.2 0.6 broadcast_multiply_fusion
  53.8 5.1 %all-to-all-start.1 = ((f32[3,4,16]{2,0,1:T(4,128)}), f32[3,4,16]{2,0,1:T(4,128)S(1)}, u32[]{:S(2)}, u32[]{:S(2)}) async-start(f32[3,4,16]{2,0,1:T(4,128)} %get-tuple-element.57), calls=%async_computation.1 | async-start | bytes 16384 | tf_op jit(solution)/shard_map/all_to_all | solution.py:114
  58.9 1.9 %collective-permute-start.9 = (f32[3,6,2,128]{3,2,1,0:T(2,128)S(1)}, f32[3,6,2,128]{3,2,1,0:T(2,128)S(1)}, u32[]{:S(2)}, u32[]{:S(2)}) collective-permute-start(f32[3,6,2,128]{3,2,1,0:T(2,128)S(1)} %get-tuple-element.51), channel_id=1, source_target_pairs={{0,4},{4,8},{8,12},{12,16},{16,20},{20,24},{24,28},{1,5},{5,9},{9,... | collective-permute-start | bytes 55304 | tf_op jit(solution)/shard_map/ppermute | solution.py:19
  60.9 3.6 %collective-permute-start.8 = (f32[3,6,2,128]{3,2,1,0:T(2,128)S(1)}, f32[3,6,2,128]{3,2,1,0:T(2,128)S(1)}, u32[]{:S(2)}, u32[]{:S(2)}) collective-permute-start(f32[3,6,2,128]{3,2,1,0:T(2,128)S(1)} %get-tuple-element.50), channel_id=1, source_target_pairs={{4,0},{8,4},{12,8},{16,12},{20,16},{24,20},{28,24},{5,1},{9,5},{13... | collective-permute-start | bytes 55304 | tf_op jit(solution)/shard_map/ppermute | solution.py:20
  64.5 5.1 %all-to-all-start.3 = ((f32[3,4,16]{2,0,1:T(4,128)}), f32[3,4,16]{2,0,1:T(4,128)S(1)}, u32[]{:S(2)}, u32[]{:S(2)}) async-start(f32[3,4,16]{2,0,1:T(4,128)} %get-tuple-element.56), calls=%async_computation.3 | async-start | bytes 16384 | tf_op jit(solution)/shard_map/all_to_all | solution.py:114
  70.7 0.7 fusion.3
  71.4 0.6 pad_maximum_fusion.38
  72.0 0.8 all-to-all-done.3
  72.9 5.6 %all-to-all-start.2 = ((f32[4,3,16]{2,1,0:T(4,128)}), f32[4,3,16]{2,1,0:T(4,128)S(1)}, u32[]{:S(2)}, u32[]{:S(2)}) async-start(f32[4,3,16]{2,1,0:T(4,128)} %pad_maximum_fusion.38), calls=%async_computation.2 | async-start | bytes 16384 | tf_op jit(solution)/shard_map/all_to_all | solution.py:119
  79.0 0.6 multiply_add_fusion.2
  79.6 2.1 %all-to-all-done.2 = f32[4,3,16]{2,1,0:T(4,128)S(1)} async-done(((f32[4,3,16]{2,1,0:T(4,128)}), f32[4,3,16]{2,1,0:T(4,128)S(1)}, u32[]{:S(2)}, u32[]{:S(2)}) %all-to-all-start.2) | async-done | bytes 800 | tf_op jit(solution)/shard_map/all_to_all | solution.py:119
  81.9 3.4 %collective-permute-start.10 = (f32[3,6,12,2]{3,2,1,0:T(8,128)S(1)}, f32[3,6,12,2]{3,2,1,0:T(8,128)S(1)}, u32[]{:S(2)}, u32[]{:S(2)}) collective-permute-start(f32[3,6,12,2]{3,2,1,0:T(8,128)S(1)} %get-tuple-element.45), channel_id=1, source_target_pairs={{1,0},{2,1},{3,2},{5,4},{6,5},{7,6},{9,8},{10,9},{11,10},{13,12},{... | collective-permute-start | bytes 5192 | tf_op jit(solution)/shard_map/ppermute | solution.py:20
  85.3 2.5 %collective-permute-start.11 = (f32[3,6,12,2]{3,2,1,0:T(8,128)S(1)}, f32[3,6,12,2]{3,2,1,0:T(8,128)S(1)}, u32[]{:S(2)}, u32[]{:S(2)}) collective-permute-start(f32[3,6,12,2]{3,2,1,0:T(8,128)S(1)} %get-tuple-element.44), channel_id=1, source_target_pairs={{0,1},{1,2},{2,3},{4,5},{5,6},{6,7},{8,9},{9,10},{10,11},{12,13},{... | collective-permute-start | bytes 5192 | tf_op jit(solution)/shard_map/ppermute | solution.py:19
  87.9 1.1 collective-permute-done.10
  89.0 3.4 %collective-permute-done.11 = f32[3,6,12,2]{3,2,1,0:T(8,128)S(1)} collective-permute-done((f32[3,6,12,2]{3,2,1,0:T(8,128)S(1)}, f32[3,6,12,2]{3,2,1,0:T(8,128)S(1)}, u32[]{:S(2)}, u32[]{:S(2)}) %collective-permute-start.11) | collective-permute-done | bytes 1760 | tf_op jit(solution)/shard_map/ppermute | solution.py:19
  93.2 1.9 %collective-permute-start.12 = (f32[6,6,2,128]{3,2,1,0:T(2,128)S(1)}, f32[6,6,2,128]{3,2,1,0:T(2,128)S(1)}, u32[]{:S(2)}, u32[]{:S(2)}) collective-permute-start(f32[6,6,2,128]{3,2,1,0:T(2,128)S(1)} %get-tuple-element.43), channel_id=1, source_target_pairs={{4,0},{8,4},{12,8},{16,12},{20,16},{24,20},{28,24},{5,1},{9,5},{13... | collective-permute-start | bytes 110600 | tf_op jit(solution)/shard_map/ppermute | solution.py:20
  95.1 2.4 %collective-permute-start.13 = (f32[6,6,2,128]{3,2,1,0:T(2,128)S(1)}, f32[6,6,2,128]{3,2,1,0:T(2,128)S(1)}, u32[]{:S(2)}, u32[]{:S(2)}) collective-permute-start(f32[6,6,2,128]{3,2,1,0:T(2,128)S(1)} %get-tuple-element.42), channel_id=1, source_target_pairs={{0,4},{4,8},{8,12},{12,16},{16,20},{20,24},{24,28},{1,5},{5,9},{9,... | collective-permute-start | bytes 110600 | tf_op jit(solution)/shard_map/ppermute | solution.py:19
  97.7 1.6 %scatter_custom_fusion.1 = f32[3,1024]{0,1:T(8,128)S(1)} fusion(s32[256]{0:T(256)S(1)} %bitcast.226, f32[256,3]{1,0:T(8,128)S(1)} %bitcast.214, f32[]{:T(128)} %constant.90.clone.1), kind=kCustom, calls=%fused_computation.48 | custom fusion | flops 768 | bytes 12292 | tf_op jit(solution)/shard_map/scatter-add | solution.py:130
  99.4 1.0 collective-permute-done.13
  100.6 3.3 %collective-permute-start.14 = (f32[6,6,12,2]{3,2,1,0:T(8,128)S(1)}, f32[6,6,12,2]{3,2,1,0:T(8,128)S(1)}, u32[]{:S(2)}, u32[]{:S(2)}) collective-permute-start(f32[6,6,12,2]{3,2,1,0:T(8,128)S(1)} %get-tuple-element.39), channel_id=1, source_target_pairs={{1,0},{2,1},{3,2},{5,4},{6,5},{7,6},{9,8},{10,9},{11,10},{13,12},{... | collective-permute-start | bytes 10376 | tf_op jit(solution)/shard_map/ppermute | solution.py:20
  104.0 2.5 %collective-permute-start.15 = (f32[6,6,12,2]{3,2,1,0:T(8,128)S(1)}, f32[6,6,12,2]{3,2,1,0:T(8,128)S(1)}, u32[]{:S(2)}, u32[]{:S(2)}) collective-permute-start(f32[6,6,12,2]{3,2,1,0:T(8,128)S(1)} %get-tuple-element.38), channel_id=1, source_target_pairs={{0,1},{1,2},{2,3},{4,5},{5,6},{6,7},{8,9},{9,10},{10,11},{12,13},{... | collective-permute-start | bytes 10376 | tf_op jit(solution)/shard_map/ppermute | solution.py:19
  106.6 4.9 %collective-permute-done.14 = f32[6,6,12,2]{3,2,1,0:T(8,128)S(1)} collective-permute-done((f32[6,6,12,2]{3,2,1,0:T(8,128)S(1)}, f32[6,6,12,2]{3,2,1,0:T(8,128)S(1)}, u32[]{:S(2)}, u32[]{:S(2)}) %collective-permute-start.14) | collective-permute-done | bytes 3488 | tf_op jit(solution)/shard_map/ppermute | solution.py:20
  111.6 3.1 %collective-permute-done.15 = f32[6,6,12,2]{3,2,1,0:T(8,128)S(1)} collective-permute-done((f32[6,6,12,2]{3,2,1,0:T(8,128)S(1)}, f32[6,6,12,2]{3,2,1,0:T(8,128)S(1)}, u32[]{:S(2)}, u32[]{:S(2)}) %collective-permute-start.15) | collective-permute-done | bytes 3488 | tf_op jit(solution)/shard_map/ppermute | solution.py:19
  115.9 0.7 multiply_add_fusion
  (118 shorter events, 9.7 us)
Async XLA Ops:
  0.6 14.9 %copy-start = (f32[8,128,128]{2,1,0:T(8,128)S(1)}, f32[8,128,128]{2,1,0:T(8,128)}, u32[]{:S(2)}) copy-start(f32[8,128,128]{2,1,0:T(8,128)} %param.24) | copy-start | bytes 1572868
  0.6 6.6 %copy-start.10 = (f32[8,3,128]{2,0,1:T(8,128)S(1)}, f32[8,3,128]{2,0,1:T(8,128)}, u32[]{:S(2)}) copy-start(f32[8,3,128]{2,0,1:T(8,128)} %param.25) | copy-start | bytes 36868
  1.7 14.6 %collective-permute-start.1 = (f32[3,6,2,128]{3,2,1,0:T(2,128)S(1)}, f32[3,6,2,128]{3,2,1,0:T(2,128)S(1)}, u32[]{:S(2)}, u32[]{:S(2)}) collective-permute-start(f32[3,6,2,128]{3,2,1,0:T(2,128)S(1)} %get-tuple-element.55), channel_id=1, source_target_pairs={{0,4},{4,8},{8,12},{12,16},{16,20},{20,24},{24,28},{1,5},{5,9},{9,... | collective-permute-start | bytes 55304 | tf_op jit(solution)/shard_map/ppermute | solution.py:19
  3.6 12.6 %collective-permute-start = (f32[3,6,2,128]{3,2,1,0:T(2,128)S(1)}, f32[3,6,2,128]{3,2,1,0:T(2,128)S(1)}, u32[]{:S(2)}, u32[]{:S(2)}) collective-permute-start(f32[3,6,2,128]{3,2,1,0:T(2,128)S(1)} %get-tuple-element.54), channel_id=1, source_target_pairs={{4,0},{8,4},{12,8},{16,12},{20,16},{24,20},{28,24},{5,1},{9,5},{13... | collective-permute-start | bytes 55304 | tf_op jit(solution)/shard_map/ppermute | solution.py:20
  7.3 0.8 copy-start.4
  7.3 0.7 copy-start.12
  8.9 15.4 %all-to-all-start = ((f32[4,3,16]{2,1,0:T(4,128)}), f32[4,3,16]{2,1,0:T(4,128)S(1)}, u32[]{:S(2)}, u32[]{:S(2)}) async-start(f32[4,3,16]{2,1,0:T(4,128)} %pad_maximum_fusion.37), calls=%async_computation | async-start | bytes 16384 | tf_op jit(solution)/shard_map/all_to_all | solution.py:119
  14.9 0.7 copy-start.11
  15.5 0.9 copy-start.2
  16.6 7.8 %collective-permute-start.3 = (f32[3,6,12,2]{3,2,1,0:T(8,128)S(1)}, f32[3,6,12,2]{3,2,1,0:T(8,128)S(1)}, u32[]{:S(2)}, u32[]{:S(2)}) collective-permute-start(f32[3,6,12,2]{3,2,1,0:T(8,128)S(1)} %get-tuple-element.48), channel_id=1, source_target_pairs={{0,1},{1,2},{2,3},{4,5},{5,6},{6,7},{8,9},{9,10},{10,11},{12,13},{... | collective-permute-start | bytes 5192 | tf_op jit(solution)/shard_map/ppermute | solution.py:19
  19.9 7.0 %collective-permute-start.2 = (f32[3,6,12,2]{3,2,1,0:T(8,128)S(1)}, f32[3,6,12,2]{3,2,1,0:T(8,128)S(1)}, u32[]{:S(2)}, u32[]{:S(2)}) collective-permute-start(f32[3,6,12,2]{3,2,1,0:T(8,128)S(1)} %get-tuple-element.49), channel_id=1, source_target_pairs={{1,0},{2,1},{3,2},{5,4},{6,5},{7,6},{9,8},{10,9},{11,10},{13,12},{... | collective-permute-start | bytes 5192 | tf_op jit(solution)/shard_map/ppermute | solution.py:20
  22.4 0.7 slice-start
  27.6 0.7 copy-start.1
  27.6 0.7 copy-start.7
  28.4 6.2 %collective-permute-start.4 = (f32[6,6,2,128]{3,2,1,0:T(2,128)S(1)}, f32[6,6,2,128]{3,2,1,0:T(2,128)S(1)}, u32[]{:S(2)}, u32[]{:S(2)}) collective-permute-start(f32[6,6,2,128]{3,2,1,0:T(2,128)S(1)} %get-tuple-element.47), channel_id=1, source_target_pairs={{4,0},{8,4},{12,8},{16,12},{20,16},{24,20},{28,24},{5,1},{9,5},{13... | collective-permute-start | bytes 110600 | tf_op jit(solution)/shard_map/ppermute | solution.py:20
  30.4 5.3 %collective-permute-start.5 = (f32[6,6,2,128]{3,2,1,0:T(2,128)S(1)}, f32[6,6,2,128]{3,2,1,0:T(2,128)S(1)}, u32[]{:S(2)}, u32[]{:S(2)}) collective-permute-start(f32[6,6,2,128]{3,2,1,0:T(2,128)S(1)} %get-tuple-element.46), channel_id=1, source_target_pairs={{0,4},{4,8},{8,12},{12,16},{16,20},{20,24},{24,28},{1,5},{5,9},{9,... | collective-permute-start | bytes 110600 | tf_op jit(solution)/shard_map/ppermute | solution.py:19
  35.9 11.7 %collective-permute-start.6 = (f32[6,6,12,2]{3,2,1,0:T(8,128)S(1)}, f32[6,6,12,2]{3,2,1,0:T(8,128)S(1)}, u32[]{:S(2)}, u32[]{:S(2)}) collective-permute-start(f32[6,6,12,2]{3,2,1,0:T(8,128)S(1)} %get-tuple-element.41), channel_id=1, source_target_pairs={{1,0},{2,1},{3,2},{5,4},{6,5},{7,6},{9,8},{10,9},{11,10},{13,12},{... | collective-permute-start | bytes 10376 | tf_op jit(solution)/shard_map/ppermute | solution.py:20
  38.3 11.6 %collective-permute-start.7 = (f32[6,6,12,2]{3,2,1,0:T(8,128)S(1)}, f32[6,6,12,2]{3,2,1,0:T(8,128)S(1)}, u32[]{:S(2)}, u32[]{:S(2)}) collective-permute-start(f32[6,6,12,2]{3,2,1,0:T(8,128)S(1)} %get-tuple-element.40), channel_id=1, source_target_pairs={{0,1},{1,2},{2,3},{4,5},{5,6},{6,7},{8,9},{9,10},{10,11},{12,13},{... | collective-permute-start | bytes 10376 | tf_op jit(solution)/shard_map/ppermute | solution.py:19
  51.1 0.9 copy-start.8
  51.2 0.9 copy-start.6
  52.0 63.9 %copy-start.3 = (f32[3,6,8,128]{3,2,1,0:T(8,128)}, f32[3,6,8,128]{3,2,1,0:T(8,128)S(1)}, u32[]{:S(2)}) copy-start(f32[3,6,8,128]{3,2,1,0:T(8,128)S(1)} %multiply_add_fusion.1) | copy-start | bytes 221188
  53.8 10.7 %all-to-all-start.1 = ((f32[3,4,16]{2,0,1:T(4,128)}), f32[3,4,16]{2,0,1:T(4,128)S(1)}, u32[]{:S(2)}, u32[]{:S(2)}) async-start(f32[3,4,16]{2,0,1:T(4,128)} %get-tuple-element.57), calls=%async_computation.1 | async-start | bytes 16384 | tf_op jit(solution)/shard_map/all_to_all | solution.py:114
  58.9 22.9 %collective-permute-start.9 = (f32[3,6,2,128]{3,2,1,0:T(2,128)S(1)}, f32[3,6,2,128]{3,2,1,0:T(2,128)S(1)}, u32[]{:S(2)}, u32[]{:S(2)}) collective-permute-start(f32[3,6,2,128]{3,2,1,0:T(2,128)S(1)} %get-tuple-element.51), channel_id=1, source_target_pairs={{0,4},{4,8},{8,12},{12,16},{16,20},{20,24},{24,28},{1,5},{5,9},{9,... | collective-permute-start | bytes 55304 | tf_op jit(solution)/shard_map/ppermute | solution.py:19
  60.9 20.9 %collective-permute-start.8 = (f32[3,6,2,128]{3,2,1,0:T(2,128)S(1)}, f32[3,6,2,128]{3,2,1,0:T(2,128)S(1)}, u32[]{:S(2)}, u32[]{:S(2)}) collective-permute-start(f32[3,6,2,128]{3,2,1,0:T(2,128)S(1)} %get-tuple-element.50), channel_id=1, source_target_pairs={{4,0},{8,4},{12,8},{16,12},{20,16},{24,20},{28,24},{5,1},{9,5},{13... | collective-permute-start | bytes 55304 | tf_op jit(solution)/shard_map/ppermute | solution.py:20
  64.5 8.4 %all-to-all-start.3 = ((f32[3,4,16]{2,0,1:T(4,128)}), f32[3,4,16]{2,0,1:T(4,128)S(1)}, u32[]{:S(2)}, u32[]{:S(2)}) async-start(f32[3,4,16]{2,0,1:T(4,128)} %get-tuple-element.56), calls=%async_computation.3 | async-start | bytes 16384 | tf_op jit(solution)/shard_map/all_to_all | solution.py:114
  69.7 0.8 copy-start.9
  70.5 8.5 %copy-start.5 = (f32[64,128]{1,0:T(8,128)}, f32[64,128]{1,0:T(8,128)S(1)}, u32[]{:S(2)}) copy-start(f32[64,128]{1,0:T(8,128)S(1)} %multiply_add_fusion.3) | copy-start | bytes 98308
  72.9 8.8 %all-to-all-start.2 = ((f32[4,3,16]{2,1,0:T(4,128)}), f32[4,3,16]{2,1,0:T(4,128)S(1)}, u32[]{:S(2)}, u32[]{:S(2)}) async-start(f32[4,3,16]{2,1,0:T(4,128)} %pad_maximum_fusion.38), calls=%async_computation.2 | async-start | bytes 16384 | tf_op jit(solution)/shard_map/all_to_all | solution.py:119
  81.9 7.0 %collective-permute-start.10 = (f32[3,6,12,2]{3,2,1,0:T(8,128)S(1)}, f32[3,6,12,2]{3,2,1,0:T(8,128)S(1)}, u32[]{:S(2)}, u32[]{:S(2)}) collective-permute-start(f32[3,6,12,2]{3,2,1,0:T(8,128)S(1)} %get-tuple-element.45), channel_id=1, source_target_pairs={{1,0},{2,1},{3,2},{5,4},{6,5},{7,6},{9,8},{10,9},{11,10},{13,12},{... | collective-permute-start | bytes 5192 | tf_op jit(solution)/shard_map/ppermute | solution.py:20
  85.3 7.0 %collective-permute-start.11 = (f32[3,6,12,2]{3,2,1,0:T(8,128)S(1)}, f32[3,6,12,2]{3,2,1,0:T(8,128)S(1)}, u32[]{:S(2)}, u32[]{:S(2)}) collective-permute-start(f32[3,6,12,2]{3,2,1,0:T(8,128)S(1)} %get-tuple-element.44), channel_id=1, source_target_pairs={{0,1},{1,2},{2,3},{4,5},{5,6},{6,7},{8,9},{9,10},{10,11},{12,13},{... | collective-permute-start | bytes 5192 | tf_op jit(solution)/shard_map/ppermute | solution.py:19
  93.2 6.2 %collective-permute-start.12 = (f32[6,6,2,128]{3,2,1,0:T(2,128)S(1)}, f32[6,6,2,128]{3,2,1,0:T(2,128)S(1)}, u32[]{:S(2)}, u32[]{:S(2)}) collective-permute-start(f32[6,6,2,128]{3,2,1,0:T(2,128)S(1)} %get-tuple-element.43), channel_id=1, source_target_pairs={{4,0},{8,4},{12,8},{16,12},{20,16},{24,20},{28,24},{5,1},{9,5},{13... | collective-permute-start | bytes 110600 | tf_op jit(solution)/shard_map/ppermute | solution.py:20
  95.1 5.3 %collective-permute-start.13 = (f32[6,6,2,128]{3,2,1,0:T(2,128)S(1)}, f32[6,6,2,128]{3,2,1,0:T(2,128)S(1)}, u32[]{:S(2)}, u32[]{:S(2)}) collective-permute-start(f32[6,6,2,128]{3,2,1,0:T(2,128)S(1)} %get-tuple-element.42), channel_id=1, source_target_pairs={{0,4},{4,8},{8,12},{12,16},{16,20},{20,24},{24,28},{1,5},{5,9},{9,... | collective-permute-start | bytes 110600 | tf_op jit(solution)/shard_map/ppermute | solution.py:19
  100.6 11.0 %collective-permute-start.14 = (f32[6,6,12,2]{3,2,1,0:T(8,128)S(1)}, f32[6,6,12,2]{3,2,1,0:T(8,128)S(1)}, u32[]{:S(2)}, u32[]{:S(2)}) collective-permute-start(f32[6,6,12,2]{3,2,1,0:T(8,128)S(1)} %get-tuple-element.39), channel_id=1, source_target_pairs={{1,0},{2,1},{3,2},{5,4},{6,5},{7,6},{9,8},{10,9},{11,10},{13,12},{... | collective-permute-start | bytes 10376 | tf_op jit(solution)/shard_map/ppermute | solution.py:20
  104.0 10.7 %collective-permute-start.15 = (f32[6,6,12,2]{3,2,1,0:T(8,128)S(1)}, f32[6,6,12,2]{3,2,1,0:T(8,128)S(1)}, u32[]{:S(2)}, u32[]{:S(2)}) collective-permute-start(f32[6,6,12,2]{3,2,1,0:T(8,128)S(1)} %get-tuple-element.38), channel_id=1, source_target_pairs={{0,1},{1,2},{2,3},{4,5},{5,6},{6,7},{8,9},{9,10},{10,11},{12,13},{... | collective-permute-start | bytes 10376 | tf_op jit(solution)/shard_map/ppermute | solution.py:19
